TPU v7x, 256 devices: a whole 4x4x8 slice. The times are simulated.
256 devices in a mesh: lat: 8 (over z_hi, core), lon: 32 (over y, z_lo, x).
Axes of the slice: x: 4, y: 4, z: 8 (z_hi: 4, z_lo: 2; z = z_hi * 2 + z_lo), core: 2. Of those that a mesh axis runs over, the one named last changes fastest.
Arguments:
- atm_state: bfloat16 [512, 1024, 384], P('lat', 'lon'), may hold values from -6 to 6
- atm_gain: float32 [384], replicated, may hold values from 0.1 to 1.9
- spec_weight: bfloat16 [2, 384, 384], replicated, may hold values from -0.21875 to 0.21875
- mlp_in: bfloat16 [384, 768], replicated, may hold values from -0.3125 to 0.3125
- mlp_out: bfloat16 [768, 384], replicated, may hold values from -0.21875 to 0.21875
- flux_weight: bfloat16 [384, 128], replicated, may hold values from -0.3125 to 0.3125
- return_weight: bfloat16 [128, 384], replicated, may hold values from -2 to 2
- ocean_state: bfloat16 [128, 512, 256], P('lat', 'lon'), may hold values from -6 to 6
- wet: int32 [128, 512], P('lat', 'lon'), may hold values 0 or 1
- ocean_in: bfloat16 [128, 256], replicated, may hold values from -0.5 to 0.5
- depth_kernel: bfloat16 [7, 7, 256], replicated, may hold values from -0.875 to 0.875
- ocean_gain: float32 [256], replicated, may hold values from 0.5 to 1.5
- ocean_up: bfloat16 [256, 1024], replicated, may hold values from -0.375 to 0.375
- ocean_down: bfloat16 [1024, 256], replicated, may hold values from -0.5 to 0.5
- surface_weight: bfloat16 [256, 128], replicated, may hold values from -0.375 to 0.375
- intersection_point: int32 [128, 512, 4], P('lat', 'lon'), may hold values from 16 to 4079, as said below
- intersection_weight: float32 [128, 512, 4], P('lat', 'lon'), may hold values from 0.1 to 1
- return_intersection: float32 [128, 512, 4], P('lat', 'lon'), may hold values from 0.1 to 1
- ocean_cot: bfloat16 [128, 512, 256], P('lat', 'lon'), may hold values from -0.15625 to 0.15625
Outputs:
- atm_next: bfloat16 [512, 1024, 384], P('lat', 'lon')
- ocean_next: bfloat16 [128, 512, 256], P('lat', 'lon')
- grad_up: float32 [256, 1024], replicated
- grad_down: float32 [1024, 256], replicated
Inputs may be any that keep to these rules, and one draw needn't show every extreme that they name: `intersection_point`: A value j < 2048 is point j (numbered row by row) of the atmosphere block at the tile's own position; a larger j is point j - 2048 of the block one device further along lon (wrapping), always in that block's first 16 columns.
All inputs are finite; a program needn't handle non-finite values. No bound on the sum of `wet` on one device may be relied on, other than what follows from the above.
Results may differ from a plain program's by a relative error of at most 0.015.
Values may be sent and summed in bfloat16 or wider, within the bound.
No kernel may reach another device: no remote copies, remote signals or barrier semaphores. Data moves between devices by JAX's collectives and lax.ppermute only.
A program may use at most 128 MiB of HBM per device.

v0:
```python
import math

import jax
import jax.numpy as jnp
from jax import lax
from jax.sharding import PartitionSpec as P

NLAT = 512
NLON = 1024
MW = 512


def passed_along(block, axis, distance):
    devices = range(lax.axis_size(axis))
    route = [((i - distance) % len(devices), i) for i in devices]
    return lax.ppermute(block, axis, route)


def padded_2(block, sides, width, periodic):
    for axis, dim in sides:
        count = lax.axis_size(axis)
        forward = [(i, i + 1) for i in range(count - 1)]
        if periodic:
            forward.append((count - 1, 0))
        backward = [(target, source) for source, target in forward]
        low = lax.ppermute(
            lax.slice_in_dim(block, block.shape[dim] - width, None, axis=dim), axis, forward
        )
        high = lax.ppermute(lax.slice_in_dim(block, 0, width, axis=dim), axis, backward)
        block = jnp.concatenate([low, block, high], axis=dim)
    return block


def dft_forward(lon_total, wave_total):
    longitude = jnp.arange(lon_total, dtype=jnp.int32)[:, None]
    wavenum = jnp.arange(wave_total, dtype=jnp.int32)[None, :]
    phases = (longitude * wavenum % lon_total).astype(jnp.float32) * (2.0 * math.pi / lon_total)
    real_part = jnp.cos(phases) / lon_total
    imag_part = -jnp.sin(phases) / lon_total
    return (
        jnp.stack([real_part, imag_part], axis=-1)
        .reshape(lon_total, 2 * wave_total)
        .astype(jnp.bfloat16)
    )


def dft_inverse(wave_total, lon_total):
    wavenum = jnp.arange(wave_total, dtype=jnp.int32)[:, None]
    longitude = jnp.arange(lon_total, dtype=jnp.int32)[None, :]
    phases = (longitude * wavenum % lon_total).astype(jnp.float32) * (2.0 * math.pi / lon_total)
    factor = jnp.where(wavenum == 0, 1.0, 2.0)
    real_part = factor * jnp.cos(phases)
    imag_part = -factor * jnp.sin(phases)
    return (
        jnp.stack([real_part, imag_part], axis=1)
        .reshape(2 * wave_total, lon_total)
        .astype(jnp.bfloat16)
    )


def quad_weights(lat_total):
    colatitude = math.pi * (jnp.arange(lat_total, dtype=jnp.float32) + 0.5) / lat_total
    return 2.0 * math.pi * (math.pi / lat_total) * jnp.sin(colatitude)


def legendre(orders, lat_total, degrees):
    colatitude = math.pi * (jnp.arange(lat_total, dtype=jnp.float32) + 0.5) / lat_total
    cosine = jnp.cos(colatitude)
    sine_vals = jnp.sin(colatitude)
    order_f = orders.astype(jnp.float32)[:, None]
    counter = jnp.arange(1, degrees, dtype=jnp.float32)[None, :]
    halves = jnp.log((2.0 * counter - 1.0) / (2.0 * counter))
    partial_log = jnp.sum(jnp.where(counter <= order_f, halves, 0.0), axis=1, keepdims=True)
    log_start = (
        0.5 * jnp.log((2.0 * order_f + 1.0) / (4.0 * math.pi))
        + 0.5 * partial_log
        + order_f * jnp.log(sine_vals)[None, :]
    )
    cos_b = cosine[None, :]
    first_step = jnp.sqrt(2.0 * order_f + 3.0) * cos_b

    def block(carry, block_id):
        older, newer = carry
        rows_out = []
        for step in range(32):
            degree_f = (block_id * 32 + step).astype(jnp.float32)
            active = degree_f >= order_f + 2.0
            coef_a = jnp.sqrt(
                jnp.where(active, 4.0 * degree_f * degree_f - 1.0, 1.0)
                / jnp.where(active, degree_f * degree_f - order_f * order_f, 1.0)
            )
            coef_b = jnp.sqrt(
                jnp.where(active, (degree_f - 1.0) * (degree_f - 1.0) - order_f * order_f, 0.0)
                / jnp.where(active, 4.0 * (degree_f - 1.0) * (degree_f - 1.0) - 1.0, 1.0)
            )
            recurred = coef_a * (cos_b * newer - coef_b * older)
            start_vals = jnp.where(
                degree_f == order_f + 1.0, first_step, jnp.where(degree_f == order_f, 1.0, 0.0)
            )
            value = jnp.where(active, recurred, start_vals)
            older, newer = (newer, value)
            rows_out.append(value)
        return ((older, newer), jnp.stack(rows_out))

    zeros_init = jnp.zeros((orders.shape[0], lat_total), jnp.float32)
    carry_out, stacked = lax.scan(
        block, (zeros_init, zeros_init), jnp.arange(degrees // 32, dtype=jnp.int32)
    )
    ratios = stacked.reshape(degrees, orders.shape[0], lat_total)
    values = ratios * jnp.exp(log_start)[None]
    values = jnp.where(log_start[None] > -70.0, values, 0.0)
    return jnp.transpose(values, (1, 0, 2))


def complex_matrix(weights):
    real_part = weights[0]
    imag_part = weights[1]
    upper_half = jnp.concatenate([real_part, imag_part], axis=1)
    lower_half = jnp.concatenate([-imag_part, real_part], axis=1)
    return jnp.concatenate([upper_half, lower_half], axis=0)


def depthwise(padded, kernel, height, breadth):
    running = jnp.zeros((height, breadth, kernel.shape[2]), jnp.float32)
    for row_off in range(7):
        for col_off in range(7):
            running = running + padded[
                row_off : row_off + height, col_off : col_off + breadth
            ].astype(jnp.float32) * kernel[row_off, col_off].astype(jnp.float32)
    return running


def layer_norm(values, gain):
    mean_val = jnp.mean(values, axis=-1, keepdims=True)
    centred = values - mean_val
    variance = jnp.mean(centred * centred, axis=-1, keepdims=True)
    return (centred * lax.rsqrt(variance + 1e-06) * gain).astype(jnp.bfloat16)


def local(
    atm_state,
    atm_gain,
    spec_weight,
    mlp_in,
    mlp_out,
    flux_weight,
    return_weight,
    ocean_state,
    wet,
    ocean_in,
    depth_kernel,
    ocean_gain,
    ocean_up,
    ocean_down,
    surface_weight,
    intersection_point,
    intersection_weight,
    return_intersection,
    ocean_cot,
):
    lat_rows, lon_cols, channels_atm = atm_state.shape
    lon_count = lax.axis_size("lon")
    lat_count = lax.axis_size("lat")
    lat_index = lax.axis_index("lat")
    lon_index = lax.axis_index("lon")
    forward_table = dft_forward(NLON, MW)
    inverse_table = dft_inverse(MW, NLON)
    state_f = atm_state.astype(jnp.float32)
    normed = (
        state_f * lax.rsqrt(jnp.mean(state_f * state_f, axis=-1, keepdims=True) + 1e-06) * atm_gain
    ).astype(jnp.bfloat16)
    spectra = jnp.einsum(
        "alc,lk->akc",
        lax.all_to_all(normed, "lon", split_axis=0, concat_axis=1, tiled=True),
        forward_table,
        preferred_element_type=jnp.float32,
    ).astype(jnp.bfloat16)
    wave_rows = lax.all_to_all(spectra, "lon", split_axis=1, concat_axis=0, tiled=True)
    by_order = lax.all_to_all(wave_rows, "lat", split_axis=1, concat_axis=0, tiled=True)
    order_count = MW // (lon_count * lat_count)
    orders = (
        lon_index * (MW // lon_count)
        + lat_index * order_count
        + jnp.arange(order_count, dtype=jnp.int32)
    )
    legendre_tab = legendre(orders, NLAT, MW)
    analysis = (legendre_tab * quad_weights(NLAT)).astype(jnp.bfloat16)
    synthesis = legendre_tab.astype(jnp.bfloat16)
    spectra_in = by_order.reshape(NLAT, order_count, 2 * channels_atm)
    coeffs = jnp.einsum(
        "mlj,jmx->lmx", analysis, spectra_in, preferred_element_type=jnp.float32
    ).astype(jnp.bfloat16)
    mixed_coef = (
        jnp.dot(
            coeffs.reshape(MW * order_count, 2 * channels_atm),
            complex_matrix(spec_weight),
            preferred_element_type=jnp.float32,
        )
        .astype(jnp.bfloat16)
        .reshape(MW, order_count, 2 * channels_atm)
    )
    grid_waves = (
        jnp.einsum("mlj,lmx->jmx", synthesis, mixed_coef, preferred_element_type=jnp.float32)
        .astype(jnp.bfloat16)
        .reshape(NLAT, 2 * order_count, channels_atm)
    )
    by_lat = lax.all_to_all(grid_waves, "lat", split_axis=0, concat_axis=1, tiled=True)
    values = jnp.einsum(
        "akc,kl->alc",
        lax.all_to_all(by_lat, "lon", split_axis=0, concat_axis=1, tiled=True),
        inverse_table,
        preferred_element_type=jnp.float32,
    ).astype(jnp.bfloat16)
    spectral = lax.all_to_all(values, "lon", split_axis=1, concat_axis=0, tiled=True)
    cell_count = lat_rows * lon_cols
    hidden = (
        (state_f + spectral.astype(jnp.float32))
        .astype(jnp.bfloat16)
        .reshape(cell_count, channels_atm)
    )
    activation = jax.nn.gelu(jnp.dot(hidden, mlp_in, preferred_element_type=jnp.float32)).astype(
        jnp.bfloat16
    )
    update = jnp.dot(activation, mlp_out, preferred_element_type=jnp.float32)
    flux_rows = jnp.dot(
        atm_state.reshape(cell_count, channels_atm), flux_weight, preferred_element_type=jnp.float32
    ).astype(jnp.bfloat16)
    field_count = flux_rows.shape[1]
    o_rows, o_cols, channels = ocean_state.shape
    ocean_cells = o_rows * o_cols
    intersections = intersection_point.shape[2]
    point_list = intersection_point.reshape(ocean_cells, intersections)
    pool_size = 2 * cell_count
    from_east = passed_along(flux_rows, "lon", -1)
    pool = jnp.concatenate([flux_rows, from_east], axis=0)
    arrived = jnp.take(pool, point_list.reshape(-1), axis=0).reshape(
        ocean_cells, intersections, field_count
    )
    forcing = jnp.sum(
        intersection_weight.reshape(ocean_cells, intersections, 1) * arrived.astype(jnp.float32),
        axis=1,
    ).astype(jnp.bfloat16)
    wet_f = wet.astype(jnp.float32).reshape(o_rows, o_cols, 1)
    ocean_mix = (
        (
            ocean_state.astype(jnp.float32)
            + jnp.dot(forcing, ocean_in, preferred_element_type=jnp.float32).reshape(
                o_rows, o_cols, channels
            )
        )
        * wet_f
    ).astype(jnp.bfloat16)
    side_ext = padded_2(ocean_mix, (("lon", 1),), 3, True)
    framed = padded_2(side_ext, (("lat", 0),), 3, False)
    top_band = lax.all_gather(ocean_mix[o_rows - 3 :], "lon", axis=1, tiled=True)
    total_cols = o_cols * lon_count
    columns = (lon_index * o_cols - 3 + jnp.arange(o_cols + 6, dtype=jnp.int32)) % total_cols
    folded = jnp.take(top_band[::-1], total_cols - 1 - columns, axis=1)
    north_rows = jnp.where(lat_index == lat_count - 1, folded, framed[o_rows + 3 :])
    padded = jnp.concatenate([framed[: o_rows + 3], north_rows], axis=0)
    depth_sum = depthwise(padded, depth_kernel, o_rows, o_cols)
    normal = layer_norm(depth_sum, ocean_gain).reshape(ocean_cells, channels)
    pre = jnp.dot(normal, ocean_up, preferred_element_type=jnp.float32)
    lifted = jax.nn.gelu(pre).astype(jnp.bfloat16)
    ocean_next = (
        (
            ocean_mix.astype(jnp.float32)
            + jnp.dot(lifted, ocean_down, preferred_element_type=jnp.float32).reshape(
                o_rows, o_cols, channels
            )
        )
        * wet_f
    ).astype(jnp.bfloat16)
    masked_cot = (
        (ocean_cot.astype(jnp.float32) * wet_f).astype(jnp.bfloat16).reshape(ocean_cells, channels)
    )
    down_local = lax.dot_general(
        lifted, masked_cot, (((0,), (0,)), ((), ())), preferred_element_type=jnp.float32
    )
    back_hidden = lax.dot_general(
        masked_cot, ocean_down, (((1,), (1,)), ((), ())), preferred_element_type=jnp.float32
    )
    gelu_out, pullback = jax.vjp(jax.nn.gelu, pre)
    pre_grad = pullback(back_hidden)[0].astype(jnp.bfloat16)
    up_local = lax.dot_general(
        normal, pre_grad, (((0,), (0,)), ((), ())), preferred_element_type=jnp.float32
    )
    grad_up, grad_down = lax.psum((up_local, down_local), ("lat", "lon"))
    surface = (
        jnp.dot(
            ocean_state.reshape(ocean_cells, channels),
            surface_weight,
            preferred_element_type=jnp.float32,
        )
        * wet.astype(jnp.float32).reshape(ocean_cells, 1)
    ).astype(jnp.bfloat16)
    terms = (
        return_intersection.reshape(ocean_cells, intersections, 1)
        * surface.astype(jnp.float32)[:, None, :]
    ).reshape(ocean_cells * intersections, field_count)
    partial_value = jax.ops.segment_sum(
        terms, point_list.reshape(-1), num_segments=pool_size
    ).astype(jnp.bfloat16)
    own_part = lax.optimization_barrier(partial_value[:cell_count])
    from_west = passed_along(partial_value[cell_count:], "lon", 1)
    returned = (own_part.astype(jnp.float32) + from_west.astype(jnp.float32)).astype(jnp.bfloat16)
    atm_next = (
        (
            hidden.astype(jnp.float32)
            + update
            + jnp.dot(returned, return_weight, preferred_element_type=jnp.float32)
        )
        .astype(jnp.bfloat16)
        .reshape(lat_rows, lon_cols, channels_atm)
    )
    return (atm_next, ocean_next, grad_up, grad_down)


def solution(mesh):
    in_specs = (
        P("lat", "lon", None),
        P(),
        P(),
        P(),
        P(),
        P(),
        P(),
        P("lat", "lon", None),
        P("lat", "lon"),
        P(),
        P(),
        P(),
        P(),
        P(),
        P(),
        P("lat", "lon", None),
        P("lat", "lon", None),
        P("lat", "lon", None),
        P("lat", "lon", None),
    )
    out_specs = (P("lat", "lon", None), P("lat", "lon", None), P(), P())
    return jax.shard_map(local, mesh=mesh, in_specs=in_specs, out_specs=out_specs, check_vma=False)
```

profile of v0, /device:TPU:1, one launch (start us, length us, event | category | flops | bytes accessed | tf_op | source)
XLA Modules:
  0.0 719.8 jit_solution(17716208627618865004)
XLA Ops:
  11.4 9.3 %all-to-all-start = ((bf16[64,32,384]{2,1,0:T(8,128)(2,1)}), bf16[64,32,384]{2,1,0:T(8,128)(2,1)}, u32[]{:S(2)}, u32[]{:S(2)}) async-start(bf16[64,32,384]{2,1,0:T(8,128)(2,1)} %fusion.212), calls=%async_computation | async-start | bytes 3145728 | tf_op jit(solution)/shard_map/all_to_all | solution.py:174
  20.8 8.6 %multiply_convert_fusion.1 = (bf16[1024,512,1]{1,0,2:T(8,128)(2,1)S(1)}, bf16[1024,512,1]{1,0,2:T(8,128)(2,1)S(1)}) fusion(), kind=kLoop, calls=%fused_computation.473 | loop fusion | flops 9961472 | bytes 2097152 | tf_op jit(solution)/shard_map/convert.53
  30.9 6.2 copy.221
  48.3 7.4 %all-to-all-start.1 = ((bf16[2,1024,384]{2,0,1:T(2,128)(2,1)}), bf16[2,1024,384]{2,0,1:T(2,128)(2,1)}, u32[]{:S(2)}, u32[]{:S(2)}) async-start(bf16[2,1024,384]{2,0,1:T(2,128)(2,1)} %copy.223), calls=%async_computation.1 | async-start | bytes 3145728 | tf_op jit(solution)/shard_map/all_to_all | solution.py:178
  55.8 20.4 %all-to-all-done.1 = bf16[2,1024,384]{2,0,1:T(2,128)(2,1)} async-done(((bf16[2,1024,384]{2,0,1:T(2,128)(2,1)}), bf16[2,1024,384]{2,0,1:T(2,128)(2,1)}, u32[]{:S(2)}, u32[]{:S(2)}) %all-to-all-start.1) | async-done | bytes 1572896 | tf_op jit(solution)/shard_map/all_to_all | solution.py:178
  79.9 10.9 %all-to-all-start.2 = ((bf16[64,32,384]{2,0,1:T(8,128)(2,1)}), bf16[64,32,384]{2,0,1:T(8,128)(2,1)}, u32[]{:S(2)}, u32[]{:S(2)}) async-start(bf16[64,32,384]{2,0,1:T(8,128)(2,1)} %copy.226), calls=%async_computation.2 | async-start | bytes 3145728 | tf_op jit(solution)/shard_map/all_to_all | solution.py:179
  90.8 100.5 %while.21 = (s32[]{:T(128)}, f32[2,512]{1,0:T(2,128)S(1)}, f32[2,512]{1,0:T(2,128)S(1)}, f32[16,32,2,512]{3,2,1,0:T(2,128)}, s32[16]{0:T(128)S(1)}, /*index=5*/s...) while((s32[]{:T(128)}, f32[2,512]{1,0:T(2,128)S(1)}, ...), condition=%wide.region_3.4_spmd.clone.clone.clone.clone, body=%wide.region_2.3_spmd.clone.clone.clone.clone.sunk | while | flops 235074 | bytes 1021500 | solution.py:106
  196.4 4.7 reshape.2776
  206.9 4.7 reshape.2778
  215.6 4.7 reshape.2779
  220.2 4.3 convolution_convert_fusion.2
  228.3 7.3 %all-to-all-start.3 = ((bf16[512,4,384]{2,1,0:T(4,128)(2,1)}), bf16[512,4,384]{2,1,0:T(4,128)(2,1)}, u32[]{:S(2)}, u32[]{:S(2)}) async-start(bf16[512,4,384]{2,1,0:T(4,128)(2,1)} %copy.232), calls=%async_computation.3 | async-start | bytes 3145728 | tf_op jit(solution)/shard_map/all_to_all | solution.py:207
  236.7 7.9 %scatter_custom_fusion = f32[4096,128]{1,0:T(8,128)} fusion(s32[1024]{0:T(1024)S(1)} %reshape.2858, f32[]{:T(128)} %constant.486.clone.1, f32[1024,128]{1,0:T(8,128)S(1)} %bitcast.1184, f32[1024]{0:T(1024)S(1)} %mul.4259), kind=kCustom, calls=%fused_computation.519 | custom fusion | flops 262144 | bytes 2625540 | tf_op jit(solution)/shard_map/scatter-add | solution.py:301
  250.3 4.3 collective-permute-start.1
  254.7 9.4 %multiply_convert_fusion.3 = (bf16[512,1,1024]{2,0,1:T(8,128)(2,1)S(1)}, bf16[512,1,1024]{2,0,1:T(8,128)(2,1)}) fusion(f32[512]{0:T(512)S(1)} %fusion.323, f32[512]{0:T(512)S(1)} %fusion.322), kind=kLoop, calls=%fused_computation.477 | loop fusion | flops 9437184 | bytes 2101248 | tf_op jit(solution)/shard_map/convert.55
  264.0 8.5 %all-to-all-done.3 = bf16[512,4,384]{2,1,0:T(4,128)(2,1)} async-done(((bf16[512,4,384]{2,1,0:T(4,128)(2,1)}), bf16[512,4,384]{2,1,0:T(4,128)(2,1)}, u32[]{:S(2)}, u32[]{:S(2)}) %all-to-all-start.3) | async-done | bytes 1572896 | tf_op jit(solution)/shard_map/all_to_all | solution.py:207
  276.4 8.0 %all-to-all-start.4 = ((bf16[64,32,384]{2,1,0:T(8,128)(2,1)}), bf16[64,32,384]{2,1,0:T(8,128)(2,1)}, u32[]{:S(2)}, u32[]{:S(2)}) async-start(bf16[64,32,384]{2,1,0:T(8,128)(2,1)} %copy.235), calls=%async_computation.4 | async-start | bytes 3145728 | tf_op jit(solution)/shard_map/all_to_all | solution.py:210
  299.3 5.8 collective-permute-start.3
  305.6 5.1 copy.220
  326.0 7.7 %all-to-all-start.5 = ((bf16[2,1024,384]{2,0,1:T(2,128)(2,1)}), bf16[2,1024,384]{2,0,1:T(2,128)(2,1)}, u32[]{:S(2)}, u32[]{:S(2)}) async-start(bf16[2,1024,384]{2,0,1:T(2,128)(2,1)} %copy.238), calls=%async_computation.5 | async-start | bytes 3145728 | tf_op jit(solution)/shard_map/all_to_all | solution.py:214
  333.8 85.5 %all_gather.3 = bf16[3,512,256]{2,1,0:T(8,128)(2,1)S(1)} all-gather(bf16[3,16,256]{2,1,0:T(8,128)(2,1)S(1)} %copy.250), channel_id=1, replica_groups=mesh['lat'=8,'lon'=32] {'lon'}, dimensions={1}, use_global_device_ids=true | all-gather | bytes 811008 | tf_op jit(solution)/shard_map/all_gather | solution.py:255
  425.7 15.5 %collective-permute-start.4 = (bf16[3,22,256]{2,0,1:T(4,128)(2,1)S(1)}, bf16[3,22,256]{2,0,1:T(4,128)(2,1)S(1)}, u32[]{:S(2)}, u32[]{:S(2)}) collective-permute-start(bf16[3,22,256]{2,0,1:T(4,128)(2,1)S(1)} %get-tuple-element.805), channel_id=1, source_target_pairs={{0,32},{32,64},{64,96},{96,128},{128,160},{160,192},{192,224},{1,3... | collective-permute-start | bytes 101384 | tf_op jit(solution)/shard_map/ppermute | solution.py:26
  457.8 7.0 fusion.214
  468.6 240.6 %all-reduce.3.cloned.1.call-done = (f32[256,1024]{1,0:T(8,128)}, f32[1024,256]{1,0:T(8,128)}) async-done(((f32[256,1024]{1,0:T(8,128)}, f32[1024,256]{1,0:T(8,128)}), (f32[256,1024]{1,0:T(8,128)}, f32[1024,256]{1,0:T(8,128)})) %all-reduce.3.cloned.1.call-update) | async-done | bytes 2097168 | tf_op jit(solution)/shard_map/psum | solution.py:288
  (2016 shorter events, 190.8 us)
Async XLA Ops:
  7.2 450.6 %copy-start = (bf16[768,384]{1,0:T(8,128)(2,1)S(1)}, bf16[768,384]{1,0:T(8,128)(2,1)}, u32[]{:S(2)}) copy-start(bf16[768,384]{1,0:T(8,128)(2,1)} %param.25) | copy-start | bytes 1769476
  11.4 30.2 %all-to-all-start = ((bf16[64,32,384]{2,1,0:T(8,128)(2,1)}), bf16[64,32,384]{2,1,0:T(8,128)(2,1)}, u32[]{:S(2)}, u32[]{:S(2)}) async-start(bf16[64,32,384]{2,1,0:T(8,128)(2,1)} %fusion.212), calls=%async_computation | async-start | bytes 3145728 | tf_op jit(solution)/shard_map/all_to_all | solution.py:174
  48.3 28.0 %all-to-all-start.1 = ((bf16[2,1024,384]{2,0,1:T(2,128)(2,1)}), bf16[2,1024,384]{2,0,1:T(2,128)(2,1)}, u32[]{:S(2)}, u32[]{:S(2)}) async-start(bf16[2,1024,384]{2,0,1:T(2,128)(2,1)} %copy.223), calls=%async_computation.1 | async-start | bytes 3145728 | tf_op jit(solution)/shard_map/all_to_all | solution.py:178
  79.9 112.8 %all-to-all-start.2 = ((bf16[64,32,384]{2,0,1:T(8,128)(2,1)}), bf16[64,32,384]{2,0,1:T(8,128)(2,1)}, u32[]{:S(2)}, u32[]{:S(2)}) async-start(bf16[64,32,384]{2,0,1:T(8,128)(2,1)} %copy.226), calls=%async_computation.2 | async-start | bytes 3145728 | tf_op jit(solution)/shard_map/all_to_all | solution.py:179
  90.8 101.0 %copy-start.6 = (bf16[2,384,384]{2,1,0:T(8,128)(2,1)S(1)}, bf16[2,384,384]{2,1,0:T(8,128)(2,1)}, u32[]{:S(2)}) copy-start(bf16[2,384,384]{2,1,0:T(8,128)(2,1)} %param.23) | copy-start | bytes 1769476
  228.3 8.1 %copy-start.16 = (bf16[256,128]{1,0:T(8,128)(2,1)S(1)}, bf16[256,128]{1,0:T(8,128)(2,1)}, u32[]{:S(2)}) copy-start(bf16[256,128]{1,0:T(8,128)(2,1)} %param.35) | copy-start | bytes 196612
  228.3 44.2 %all-to-all-start.3 = ((bf16[512,4,384]{2,1,0:T(4,128)(2,1)}), bf16[512,4,384]{2,1,0:T(4,128)(2,1)}, u32[]{:S(2)}, u32[]{:S(2)}) async-start(bf16[512,4,384]{2,1,0:T(4,128)(2,1)} %copy.232), calls=%async_computation.3 | async-start | bytes 3145728 | tf_op jit(solution)/shard_map/all_to_all | solution.py:207
  247.5 217.3 %collective-permute-start = (bf16[2048,128]{1,0:T(8,128)(2,1)}, bf16[2048,128]{1,0:T(8,128)(2,1)}, u32[]{:S(2)}, u32[]{:S(2)}) collective-permute-start(bf16[2048,128]{1,0:T(8,128)(2,1)} %get-tuple-element.800), channel_id=1, source_target_pairs={{31,0},{0,1},{1,2},{2,3},{3,4},{4,5},{5,6},{6,7},{7,8},{8,9},{9,10... | collective-permute-start | bytes 1572872 | tf_op jit(solution)/shard_map/ppermute | solution.py:16
  250.3 40.1 %collective-permute-start.1 = (bf16[2048,128]{1,0:T(8,128)(2,1)}, bf16[2048,128]{1,0:T(8,128)(2,1)}, u32[]{:S(2)}, u32[]{:S(2)}) collective-permute-start(bf16[2048,128]{1,0:T(8,128)(2,1)} %convolution_convert_fusion), channel_id=1, source_target_pairs={{1,0},{2,1},{3,2},{4,3},{5,4},{6,5},{7,6},{8,7},{9,8},{10,9},{11,1... | collective-permute-start | bytes 1572872 | tf_op jit(solution)/shard_map/ppermute | solution.py:16
  276.4 8.2 %copy-start.18 = (f32[16,16,4]{1,2,0:T(4,128)S(1)}, f32[16,16,4]{1,2,0:T(4,128)}, u32[]{:S(2)}) copy-start(f32[16,16,4]{1,2,0:T(4,128)} %param.37) | copy-start | bytes 12292
  276.4 42.8 %all-to-all-start.4 = ((bf16[64,32,384]{2,1,0:T(8,128)(2,1)}), bf16[64,32,384]{2,1,0:T(8,128)(2,1)}, u32[]{:S(2)}, u32[]{:S(2)}) async-start(bf16[64,32,384]{2,1,0:T(8,128)(2,1)} %copy.235), calls=%async_computation.4 | async-start | bytes 3145728 | tf_op jit(solution)/shard_map/all_to_all | solution.py:210
  299.3 15.5 %collective-permute-start.3 = (bf16[16,3,256]{2,0,1:T(8,128)(2,1)S(1)}, bf16[16,3,256]{2,0,1:T(8,128)(2,1)S(1)}, u32[]{:S(2)}, u32[]{:S(2)}) collective-permute-start(bf16[16,3,256]{2,0,1:T(8,128)(2,1)S(1)} %get-tuple-element.808), channel_id=1, source_target_pairs={{1,0},{2,1},{3,2},{4,3},{5,4},{6,5},{7,6},{8,7},{9,8},{10,9},{11,1... | collective-permute-start | bytes 73736 | tf_op jit(solution)/shard_map/ppermute | solution.py:29
  305.1 9.8 %collective-permute-start.2 = (bf16[16,3,256]{2,0,1:T(8,128)(2,1)S(1)}, bf16[16,3,256]{2,0,1:T(8,128)(2,1)S(1)}, u32[]{:S(2)}, u32[]{:S(2)}) collective-permute-start(bf16[16,3,256]{2,0,1:T(8,128)(2,1)S(1)} %get-tuple-element.807), channel_id=1, source_target_pairs={{0,1},{1,2},{2,3},{3,4},{4,5},{5,6},{6,7},{7,8},{8,9},{9,10},{10,1... | collective-permute-start | bytes 73736 | tf_op jit(solution)/shard_map/ppermute | solution.py:26
  315.5 125.8 %collective-permute-start.5 = (bf16[3,22,256]{2,0,1:T(4,128)(2,1)}, bf16[3,22,256]{2,0,1:T(4,128)(2,1)S(1)}, u32[]{:S(2)}, u32[]{:S(2)}) collective-permute-start(bf16[3,22,256]{2,0,1:T(4,128)(2,1)} %get-tuple-element.806), channel_id=1, source_target_pairs={{32,0},{64,32},{96,64},{128,96},{160,128},{192,160},{224,192},{33,... | collective-permute-start | bytes 101384 | tf_op jit(solution)/shard_map/ppermute | solution.py:29
  326.0 126.9 %all-to-all-start.5 = ((bf16[2,1024,384]{2,0,1:T(2,128)(2,1)}), bf16[2,1024,384]{2,0,1:T(2,128)(2,1)}, u32[]{:S(2)}, u32[]{:S(2)}) async-start(bf16[2,1024,384]{2,0,1:T(2,128)(2,1)} %copy.238), calls=%async_computation.5 | async-start | bytes 3145728 | tf_op jit(solution)/shard_map/all_to_all | solution.py:214
  333.8 375.4 %all-reduce.3.cloned.1.call-start = ((), (), s32[]{:S(2)}) async-start(), calls=%async_computation.6 | async-start | bytes 4194304 | tf_op jit(solution)/shard_map/psum | solution.py:288
  420.0 22.3 %copy-start.20 = (f32[1,1,256]{2,1,0:T(1,128)S(1)}, f32[1,1,256]{2,1,0:T(1,128)}, u32[]{:S(2)}) copy-start(f32[1,1,256]{2,1,0:T(1,128)} %get-tuple-element.855) | copy-start | bytes 3076
  420.0 22.3 %copy-start.21 = (f32[1,1,256]{2,1,0:T(1,128)S(1)}, f32[1,1,256]{2,1,0:T(1,128)}, u32[]{:S(2)}) copy-start(f32[1,1,256]{2,1,0:T(1,128)} %get-tuple-element.856) | copy-start | bytes 3076
  420.0 22.3 %copy-start.22 = (f32[1,1,256]{2,1,0:T(1,128)S(1)}, f32[1,1,256]{2,1,0:T(1,128)}, u32[]{:S(2)}) copy-start(f32[1,1,256]{2,1,0:T(1,128)} %get-tuple-element.857) | copy-start | bytes 3076
  420.0 22.3 %copy-start.23 = (f32[1,1,256]{2,1,0:T(1,128)S(1)}, f32[1,1,256]{2,1,0:T(1,128)}, u32[]{:S(2)}) copy-start(f32[1,1,256]{2,1,0:T(1,128)} %get-tuple-element.809) | copy-start | bytes 3076
  420.0 22.3 %copy-start.24 = (f32[1,1,256]{2,1,0:T(1,128)S(1)}, f32[1,1,256]{2,1,0:T(1,128)}, u32[]{:S(2)}) copy-start(f32[1,1,256]{2,1,0:T(1,128)} %get-tuple-element.810) | copy-start | bytes 3076
  420.1 22.3 %copy-start.25 = (f32[1,1,256]{2,1,0:T(1,128)S(1)}, f32[1,1,256]{2,1,0:T(1,128)}, u32[]{:S(2)}) copy-start(f32[1,1,256]{2,1,0:T(1,128)} %get-tuple-element.811) | copy-start | bytes 3076
  420.1 22.3 %copy-start.26 = (f32[1,1,256]{2,1,0:T(1,128)S(1)}, f32[1,1,256]{2,1,0:T(1,128)}, u32[]{:S(2)}) copy-start(f32[1,1,256]{2,1,0:T(1,128)} %get-tuple-element.812) | copy-start | bytes 3076
  425.7 16.4 %collective-permute-start.4 = (bf16[3,22,256]{2,0,1:T(4,128)(2,1)S(1)}, bf16[3,22,256]{2,0,1:T(4,128)(2,1)S(1)}, u32[]{:S(2)}, u32[]{:S(2)}) collective-permute-start(bf16[3,22,256]{2,0,1:T(4,128)(2,1)S(1)} %get-tuple-element.805), channel_id=1, source_target_pairs={{0,32},{32,64},{64,96},{96,128},{128,160},{160,192},{192,224},{1,3... | collective-permute-start | bytes 101384 | tf_op jit(solution)/shard_map/ppermute | solution.py:26
  (19 other events, 83.4 us)
Sparse Core Ops, SparseCore 0:
  453.0 256.1 all-reduce.2
where the time goes:
time: 728 us; the launch traced here: 720 us
  waiting for transfers between devices  270 us (37%)
  other arithmetic  114 us (16%)
  local copies, waits for them, and re-layouts  99.5 us (14%)
  blocking collectives  85.5 us (12%)
  starting transfers between devices  81.5 us (11%)
  matrix products  33.6 us (5%)
  loops' own time  19.8 us (3%)
  between operations  15.3 us (2%)
    psum x1, waiting for transfers between devices, local(): grad_up, grad_down = lax.psum((up_local, down_local), ('lat', 'lon'))  241 us
    all_gather x1, blocking collectives, local(): top_band = lax.all_gather(ocean_mix[o_rows - 3:], 'lon', axis=1, tiled=True)  85.5 us
    while x496, other arithmetic  42.7 us
    all_to_all x1, waiting for transfers between devices, local(): lax.all_to_all(spectra, 'lon', split_axis=1, concat_axis=0, tiled=True)  20.4 us
    another operation x1, loops' own time, legendre(): lax.scan(block, (zeros_init, zeros_init), jnp.arange(degrees // 32, dtype...  19.8 us
    another operation x2, other arithmetic  18 us
    ppermute x2, starting transfers between devices, padded_2(): lax.ppermute(lax.slice_in_dim(block, block.shape[dim] - width, None, axis...  15.6 us
  transfers between devices with their start and end apart: 13, of which 5 were waited for; matrix products, arithmetic and copies ran while one was open for 27% of the time, Pallas kernels for 0%

commit v1 on v0

v1 whole, which is shorter than its diff:
```python
import functools
import math

import jax
import jax.numpy as jnp
import ml_dtypes
import numpy as np
from jax import lax
from jax.experimental import pallas as pl
from jax.experimental.pallas import tpu as pltpu
from jax.sharding import Mesh
from jax.sharding import PartitionSpec as P

C = 384
HID = 768
NLAT = 512
NLON = 1024
MW = 512
FL = 128
OC = 256
OH = 1024
ROWS = 64
COLS = 32
POINTS = ROWS * COLS
EAST = ROWS * 16
CELLS = 256
KOV = 4
DEV = 256
BF = jnp.bfloat16
F32 = jnp.float32
GELU_K = math.sqrt(2.0 / math.pi)

NN = (((1,), (0,)), ((), ()))
NT = (((1,), (1,)), ((), ()))
TN = (((0,), (0,)), ((), ()))


def dot(a, b, dims=NN):
    return lax.dot_general(a, b, dims, preferred_element_type=F32)


def orders_of_device():
    d = np.arange(DEV)
    return np.stack([d, MW - 1 - d], axis=1)


@functools.cache
def dft_tables():
    orders = orders_of_device().T
    lon = np.arange(NLON)
    phase = 2.0 * np.pi * ((orders[:, :, None] * lon) % NLON) / NLON
    forward = np.stack([np.cos(phase), -np.sin(phase)], axis=1) / NLON
    factor = np.where(orders == 0, 1.0, 2.0)[:, None, :, None]
    inverse = np.stack([np.cos(phase), -np.sin(phase)], axis=1) * factor
    forward = forward.reshape(2 * MW, NLON).astype(np.float32).astype(ml_dtypes.bfloat16)
    inverse = inverse.reshape(2 * MW, NLON).T.astype(np.float32).astype(ml_dtypes.bfloat16)
    return forward, np.ascontiguousarray(inverse)


@functools.cache
def legendre_constants():
    orders = orders_of_device().astype(np.float64)
    lat = np.concatenate([np.arange(0, NLAT, 2), np.arange(1, NLAT, 2)])
    theta = np.pi * (lat + 0.5) / NLAT
    k = np.arange(1, MW, dtype=np.float64)
    partial = np.concatenate([[0.0], np.cumsum(np.log((2 * k - 1) / (2 * k)))])
    partial = partial[orders_of_device()]
    log_s = (0.5 * np.log((2 * orders + 1) / (4 * np.pi)) + 0.5 * partial)[:, :, None]
    log_s = log_s + orders[:, :, None] * np.log(np.sin(theta))
    seed = np.where(log_s > -70.0, np.exp(log_s), 0.0).astype(np.float32)
    seed = seed.reshape(DEV, 8, 128)
    cosine = np.tile(np.cos(theta).astype(np.float32).reshape(4, 128), (2, 1))
    quad = (2.0 * np.pi * (np.pi / NLAT) * np.sin(theta)).astype(np.float32).reshape(4, 128)
    degree = np.arange(MW, dtype=np.float64)
    m = orders[:, :, None]
    live = degree >= m + 1
    a = np.sqrt((4 * degree**2 - 1) / np.where(live, degree**2 - m**2, 1.0), where=live, out=np.zeros(live.shape))
    b2 = np.where(live, (degree - 1) ** 2 - m**2, 0.0) / np.where(live, 4 * (degree - 1) ** 2 - 1, 1.0)
    b = np.sqrt(np.maximum(b2, 0.0))
    coef = np.concatenate([a, a * b], axis=1).astype(np.float32)
    return seed, cosine, quad, coef


def legendre_kernel(dev_ref, coef_ref, seed_ref, cos_ref, quad_ref, ana_ref, syn_ref, vals):
    dev = dev_ref[0]
    upper = lax.broadcasted_iota(jnp.int32, (8, 128), 0) < 4
    order = jnp.where(upper, dev, MW - 1 - dev)
    seed = seed_ref[0]
    cosine = cos_ref[...]

    def block(i, carry):
        older, newer = carry
        for step in range(16):
            l = i * 16 + step
            a = jnp.where(upper, coef_ref[0, 0, l], coef_ref[0, 1, l]) * cosine
            ab = jnp.where(upper, coef_ref[0, 2, l], coef_ref[0, 3, l])
            value = a * newer - ab * older
            value = jnp.where(order == l, seed, value)
            vals[pl.ds(pl.multiple_of(l * 8, 8), 8), :] = value
            older, newer = newer, value
        return older, newer

    zero = jnp.zeros((8, 128), F32)
    lax.fori_loop(0, MW // 16, block, (zero, zero))
    for m in range(2):
        for jc in range(4):
            table = vals[pl.ds(m * 4 + jc, MW, stride=8), :]
            ana_ref[m, :, jc * 128 : (jc + 1) * 128] = (table * quad_ref[jc : jc + 1, :]).astype(BF)
            syn_ref[m, :, jc * 128 : (jc + 1) * 128] = table.astype(BF)


def legendre_tables(dev):
    seed, cosine, quad, coef = legendre_constants()
    table = jax.ShapeDtypeStruct((2, MW, NLAT), BF)
    whole = lambda *shape: pl.BlockSpec(shape, lambda i, d: (0,) * len(shape))
    return pl.pallas_call(
        legendre_kernel,
        out_shape=(table, table),
        grid_spec=pltpu.PrefetchScalarGridSpec(
            num_scalar_prefetch=1,
            grid=(1,),
            in_specs=[
                pl.BlockSpec((1, 4, MW), lambda i, d: (d[0], 0, 0), memory_space=pltpu.SMEM),
                pl.BlockSpec((1, 8, 128), lambda i, d: (d[0], 0, 0)),
                whole(8, 128),
                whole(4, 128),
            ],
            out_specs=[whole(2, MW, NLAT), whole(2, MW, NLAT)],
            scratch_shapes=[pltpu.VMEM((MW * 8, 128), F32)],
        ),
        compiler_params=pltpu.CompilerParams(vmem_limit_bytes=32 << 20),
        cost_estimate=pl.CostEstimate(flops=10_000_000, bytes_accessed=4_000_000, transcendentals=0),
        name="legendre",
    )(dev, jnp.asarray(coef), jnp.asarray(seed), jnp.asarray(cosine), jnp.asarray(quad))


def norm_kernel(x_ref, gain_ref, fw_ref, msg_ref, flux_ref, west_ref):
    x = x_ref[...]
    xf = x.astype(F32)
    scale = lax.rsqrt(jnp.mean(xf * xf, axis=-1, keepdims=True) + 1e-06)
    normed = (xf * scale * gain_ref[...].reshape(1, 1, C)).astype(BF)
    pairs = normed.reshape(x.shape[0] // 2, 2, COLS, C)
    msg_ref[:, :, :C] = pairs[:, 0]
    msg_ref[:, :, C:] = pairs[:, 1]
    flux = dot(x.reshape(-1, C), fw_ref[...]).astype(BF)
    flux_ref[...] = flux
    west_ref[...] = flux.reshape(x.shape[0], 2, 16, FL)[:, 0].reshape(-1, FL)


def norm_and_flux(atm_state, gain, flux_weight):
    step = 16
    return pl.pallas_call(
        norm_kernel,
        grid=(ROWS // step,),
        out_shape=(
            jax.ShapeDtypeStruct((ROWS // 2, COLS, 2 * C), BF),
            jax.ShapeDtypeStruct((POINTS, FL), BF),
            jax.ShapeDtypeStruct((EAST, FL), BF),
        ),
        in_specs=[
            pl.BlockSpec((step, COLS, C), lambda i: (i, 0, 0)),
            pl.BlockSpec((1, C), lambda i: (0, 0)),
            pl.BlockSpec((C, FL), lambda i: (0, 0)),
        ],
        out_specs=[
            pl.BlockSpec((step // 2, COLS, 2 * C), lambda i: (i, 0, 0)),
            pl.BlockSpec((step * COLS, FL), lambda i: (i, 0)),
            pl.BlockSpec((step * 16, FL), lambda i: (i, 0)),
        ],
        compiler_params=pltpu.CompilerParams(vmem_limit_bytes=32 << 20),
        cost_estimate=pl.CostEstimate(flops=210_000_000, bytes_accessed=4_000_000, transcendentals=0),
        name="norm_flux",
    )(atm_state, gain.reshape(1, C), flux_weight)


def interleave(acc, matrix, mp):
    for a in range(2):
        for t in range(3):
            lane = a * C + t * 128
            acc[t, pl.ds(a * 4 + mp, DEV, stride=8), :] = matrix[:, lane : lane + 128]


def drain(acc, out_ref):
    for t in range(3):
        out_ref[:, :, t * 128 : (t + 1) * 128] = acc[t].reshape(DEV, 8, 128).astype(BF)


def fill(acc, in_ref):
    for t in range(3):
        acc[t] = in_ref[:, :, t * 128 : (t + 1) * 128].astype(F32).reshape(DEV * 8, 128)


def picked(acc, a, mp, t):
    return acc[t, pl.ds(a * 4 + mp, DEV, stride=8), :].astype(BF)


def dft_kernel(x_ref, table_ref, out_ref, acc):
    x = x_ref[...].reshape(NLON, 2 * C)
    for part in range(4):
        res = dot(table_ref[part * DEV : (part + 1) * DEV, :], x)
        interleave(acc, res, part)
    drain(acc, out_ref)


def dft(rows, table):
    return pl.pallas_call(
        dft_kernel,
        out_shape=jax.ShapeDtypeStruct((DEV, 8, C), BF),
        scratch_shapes=[pltpu.VMEM((3, DEV * 8, 128), F32)],
        compiler_params=pltpu.CompilerParams(vmem_limit_bytes=32 << 20),
        cost_estimate=pl.CostEstimate(flops=1_700_000_000, bytes_accessed=6_000_000, transcendentals=0),
        name="dft",
    )(rows, table)


def inverse_kernel(w_ref, table_ref, out_ref, acc, waves):
    fill(acc, w_ref)
    for part in range(4):
        for a in range(2):
            for t in range(3):
                lane = a * C + t * 128
                waves[part * DEV : (part + 1) * DEV, lane : lane + 128] = picked(acc, a, part, t)
    for t in range(4):
        res = dot(table_ref[t * 256 : (t + 1) * 256, :], waves[...])
        out_ref[t * 8 : (t + 1) * 8] = res.astype(BF).reshape(8, COLS, 2 * C)


def inverse_dft(waves, table):
    return pl.pallas_call(
        inverse_kernel,
        out_shape=jax.ShapeDtypeStruct((32, COLS, 2 * C), BF),
        scratch_shapes=[pltpu.VMEM((3, DEV * 8, 128), F32), pltpu.VMEM((2 * MW, 2 * C), BF)],
        compiler_params=pltpu.CompilerParams(vmem_limit_bytes=32 << 20),
        cost_estimate=pl.CostEstimate(flops=1_700_000_000, bytes_accessed=6_000_000, transcendentals=0),
        name="inverse_dft",
    )(waves, table)


def spectral_kernel(w_ref, ana_ref, syn_ref, sw_ref, out_ref, acc, waves, mixer):
    mixer[:C, :C] = sw_ref[0]
    mixer[:C, C:] = sw_ref[1]
    mixer[C:, :C] = -sw_ref[1]
    mixer[C:, C:] = sw_ref[0]
    fill(acc, w_ref)
    for m in range(2):
        for p in range(2):
            for a in range(2):
                for t in range(3):
                    lane = p * C + t * 128
                    waves[a * DEV : (a + 1) * DEV, lane : lane + 128] = picked(acc, a, m * 2 + p, t)
        coeff = dot(ana_ref[m], waves[...]).astype(BF)
        mixed = dot(coeff, mixer[...]).astype(BF)
        grid = dot(syn_ref[m], mixed, TN)
        for p in range(2):
            for a in range(2):
                for t in range(3):
                    lane = p * C + t * 128
                    acc[t, pl.ds(a * 4 + m * 2 + p, DEV, stride=8), :] = grid[
                        a * DEV : (a + 1) * DEV, lane : lane + 128
                    ]
    drain(acc, out_ref)


def spectral_mix(waves, analysis, synthesis, spec_weight):
    return pl.pallas_call(
        spectral_kernel,
        out_shape=jax.ShapeDtypeStruct((DEV, 8, C), BF),
        scratch_shapes=[
            pltpu.VMEM((3, DEV * 8, 128), F32),
            pltpu.VMEM((NLAT, 2 * C), BF),
            pltpu.VMEM((2 * C, 2 * C), BF),
        ],
        compiler_params=pltpu.CompilerParams(vmem_limit_bytes=40 << 20),
        cost_estimate=pl.CostEstimate(flops=2_900_000_000, bytes_accessed=6_000_000, transcendentals=0),
        name="spectral_mix",
    )(waves, analysis, synthesis, spec_weight)


def gelu_parts(x):
    t = jnp.tanh(GELU_K * (x + 0.044715 * (x * x * x)))
    return 0.5 * (1.0 + t), t


def finish_kernel(x_ref, s_ref, own_ref, west_ref, w1_ref, w2_ref, rw_ref, out_ref):
    rows = x_ref.shape[0]
    x = x_ref[...].astype(F32).reshape(rows // 2, 2, COLS, C)
    hidden = jnp.stack(
        [x[:, 0] + s_ref[:, :, :C].astype(F32), x[:, 1] + s_ref[:, :, C:].astype(F32)], axis=1
    )
    hidden = hidden.reshape(rows * COLS, C).astype(BF)
    pre = dot(hidden, w1_ref[...])
    act = (pre * gelu_parts(pre)[0]).astype(BF)
    own = own_ref[...].astype(F32).reshape(rows, 2, 16, FL)
    west = own[:, 0] + west_ref[...].astype(F32).reshape(rows, 16, FL)
    returned = jnp.stack([west, own[:, 1]], axis=1).reshape(rows * COLS, FL).astype(BF)
    out = hidden.astype(F32) + dot(act, w2_ref[...]) + dot(returned, rw_ref[...])
    out_ref[...] = out.astype(BF).reshape(rows, COLS, C)


def finish(atm_state, spectral, own, west, mlp_in, mlp_out, return_weight):
    step = 16
    return pl.pallas_call(
        finish_kernel,
        grid=(ROWS // step,),
        out_shape=jax.ShapeDtypeStruct((ROWS, COLS, C), BF),
        in_specs=[
            pl.BlockSpec((step, COLS, C), lambda i: (i, 0, 0)),
            pl.BlockSpec((step // 2, COLS, 2 * C), lambda i: (i, 0, 0)),
            pl.BlockSpec((step * COLS, FL), lambda i: (i, 0)),
            pl.BlockSpec((step * 16, FL), lambda i: (i, 0)),
            pl.BlockSpec((C, HID), lambda i: (0, 0)),
            pl.BlockSpec((HID, C), lambda i: (0, 0)),
            pl.BlockSpec((FL, C), lambda i: (0, 0)),
        ],
        out_specs=pl.BlockSpec((step, COLS, C), lambda i: (i, 0, 0)),
        compiler_params=pltpu.CompilerParams(vmem_limit_bytes=40 << 20),
        cost_estimate=pl.CostEstimate(flops=2_700_000_000, bytes_accessed=6_000_000, transcendentals=1_600_000),
        name="finish",
    )(atm_state, spectral, own, west, mlp_in, mlp_out, return_weight)


def scatter_kernel(state_ref, sw_ref, wet_ref, point_ref, weight_ref, own_ref, east_ref):
    surface = (dot(state_ref[...].reshape(CELLS, OC), sw_ref[...]) * wet_ref[...]).astype(BF)

    def spread(first, count):
        ids = first + lax.broadcasted_iota(jnp.int32, (count, CELLS), 0)
        total = jnp.zeros((count, CELLS), F32)
        for k in range(KOV):
            total = total + jnp.where(ids == point_ref[k : k + 1, :], weight_ref[k : k + 1, :], 0.0)
        return dot(total.astype(BF), surface).astype(BF)

    for i in range(4):
        own_ref[i * 512 : (i + 1) * 512, :] = spread(i * 512, 512)
    for i in range(2):
        east_ref[i * 512 : (i + 1) * 512, :] = spread(POINTS + i * 512, 512)


def scatter(ocean_state, surface_weight, wet_col, points, weights):
    return pl.pallas_call(
        scatter_kernel,
        out_shape=(
            jax.ShapeDtypeStruct((POINTS, FL), BF),
            jax.ShapeDtypeStruct((EAST, FL), BF),
        ),
        compiler_params=pltpu.CompilerParams(vmem_limit_bytes=32 << 20),
        cost_estimate=pl.CostEstimate(flops=250_000_000, bytes_accessed=1_500_000, transcendentals=0),
        name="scatter",
    )(ocean_state, surface_weight, wet_col, points, weights)


def gather_kernel(flux_ref, east_ref, state_ref, wet_ref, oin_ref, point_ref, weight_ref, out_ref):
    def pick(first, count, source):
        ids = first + lax.broadcasted_iota(jnp.int32, (CELLS, count), 1)
        total = jnp.zeros((CELLS, count), F32)
        for k in range(KOV):
            total = total + jnp.where(ids == point_ref[:, k : k + 1], weight_ref[:, k : k + 1], 0.0)
        return dot(total.astype(BF), source)

    forcing = jnp.zeros((CELLS, FL), F32)
    for i in range(4):
        forcing = forcing + pick(i * 512, 512, flux_ref[i * 512 : (i + 1) * 512, :])
    for i in range(2):
        forcing = forcing + pick(POINTS + i * 512, 512, east_ref[i * 512 : (i + 1) * 512, :])
    added = dot(forcing.astype(BF), oin_ref[...])
    state = state_ref[...].reshape(CELLS, OC).astype(F32)
    out_ref[...] = ((state + added) * wet_ref[...]).astype(BF).reshape(16, 16, OC)


def gather(flux, east, ocean_state, wet_col, ocean_in, points, weights):
    return pl.pallas_call(
        gather_kernel,
        out_shape=jax.ShapeDtypeStruct((16, 16, OC), BF),
        compiler_params=pltpu.CompilerParams(vmem_limit_bytes=32 << 20),
        cost_estimate=pl.CostEstimate(flops=250_000_000, bytes_accessed=1_500_000, transcendentals=0),
        name="gather",
    )(flux, east, ocean_state, wet_col, ocean_in, points, weights)


def ocean_kernel(
    mix_ref, west_ref, east_ref, south_ref, north_ref, dk_ref, gain_ref, up_ref, down_ref, wet_ref, cot_ref,
    next_ref, grad_ref, pad,
):
    pad[0:3] = south_ref[...].astype(F32)
    pad[3:19, 0:3] = west_ref[...].astype(F32)
    pad[3:19, 3:19] = mix_ref[...].astype(F32)
    pad[3:19, 19:22] = east_ref[...].astype(F32)
    pad[19:22] = north_ref[...].astype(F32)
    depth = jnp.zeros((16, 16, OC), F32)
    for j in range(7):
        shifted = pad[:, j : j + 16, :]
        for i in range(7):
            depth = depth + shifted[i : i + 16] * dk_ref[i * 7 + j : i * 7 + j + 1, :].astype(F32).reshape(1, 1, OC)
    depth = depth.reshape(CELLS, OC)
    centred = depth - jnp.mean(depth, axis=-1, keepdims=True)
    variance = jnp.mean(centred * centred, axis=-1, keepdims=True)
    normal = (centred * lax.rsqrt(variance + 1e-06) * gain_ref[...]).astype(BF)
    wet = wet_ref[...]
    cot = (cot_ref[...].reshape(CELLS, OC).astype(F32) * wet).astype(BF)
    total = jnp.zeros((CELLS, OC), F32)
    for h in range(4):
        cut = slice(h * 256, (h + 1) * 256)
        pre = dot(normal, up_ref[:, cut])
        half, t = gelu_parts(pre)
        lifted = (pre * half).astype(BF)
        total = total + dot(lifted, down_ref[cut, :])
        gdown = dot(lifted, cot, TN).astype(BF)
        grad_ref[h * 8 : (h + 1) * 8, 32:, :] = gdown.reshape(8, 32, OC)
        slope = half + 0.5 * pre * (1.0 - t * t) * (GELU_K * (1.0 + 3.0 * 0.044715 * (pre * pre)))
        pre_grad = (dot(cot, down_ref[cut, :], NT) * slope).astype(BF)
        gup = dot(normal, pre_grad, TN).astype(BF)
        grad_ref[:, h * 8 : (h + 1) * 8, :] = gup.reshape(32, 8, 256)
    mix = mix_ref[...].reshape(CELLS, OC).astype(F32)
    next_ref[...] = ((mix + total) * wet).astype(BF).reshape(16, 16, OC)


def ocean(mix, west, east, south, north, depth_kernel, gain, up, down, wet_col, cot):
    return pl.pallas_call(
        ocean_kernel,
        out_shape=(
            jax.ShapeDtypeStruct((16, 16, OC), BF),
            jax.ShapeDtypeStruct((32, 64, 256), BF),
        ),
        scratch_shapes=[pltpu.VMEM((22, 22, OC), F32)],
        compiler_params=pltpu.CompilerParams(vmem_limit_bytes=40 << 20),
        cost_estimate=pl.CostEstimate(flops=700_000_000, bytes_accessed=4_000_000, transcendentals=260_000),
        name="ocean",
    )(mix, west, east, south, north, depth_kernel.reshape(49, OC), gain.reshape(1, OC), up, down, wet_col, cot)


def sum_kernel(parts_ref, out_ref):
    total = parts_ref[0].astype(F32)
    for i in range(1, parts_ref.shape[0]):
        total = total + parts_ref[i].astype(F32)
    out_ref[...] = total.astype(BF)


def sum_parts(parts, name):
    return pl.pallas_call(
        sum_kernel,
        out_shape=jax.ShapeDtypeStruct(parts.shape[1:], BF),
        cost_estimate=pl.CostEstimate(flops=parts.size, bytes_accessed=parts.size * 2, transcendentals=0),
        name=name,
    )(parts)


def unpack_kernel(parts_ref, up_ref, down_ref):
    for q in range(4):
        block = parts_ref[:, q * 8 : (q + 1) * 8, :].astype(F32)
        up_ref[:, q * 256 : (q + 1) * 256] = block.reshape(256, 256)
    down_ref[...] = parts_ref[:, 32:, :].astype(F32).reshape(OH, OC)


def unpack(parts):
    return pl.pallas_call(
        unpack_kernel,
        out_shape=(jax.ShapeDtypeStruct((OC, OH), F32), jax.ShapeDtypeStruct((OH, OC), F32)),
        cost_estimate=pl.CostEstimate(flops=1_000_000, bytes_accessed=3_000_000, transcendentals=0),
        name="unpack",
    )(parts)


def exchange(x, axes):
    return lax.all_to_all(x, axes, split_axis=0, concat_axis=0, tiled=True)


def spread(x, axes, count):
    return exchange(jnp.broadcast_to(x[None], (count, *x.shape)), axes)


def after(x, *others):
    return lax.optimization_barrier((x, *others))[0]


def ring(count, distance):
    return [(i, (i + distance) % count) for i in range(count)]


def local(
    atm_state,
    atm_gain,
    spec_weight,
    mlp_in,
    mlp_out,
    flux_weight,
    return_weight,
    ocean_state,
    wet,
    ocean_in,
    depth_kernel,
    ocean_gain,
    ocean_up,
    ocean_down,
    surface_weight,
    intersection_point,
    intersection_weight,
    return_intersection,
    ocean_cot,
):
    lat = lax.axis_index(LAT)
    lon = lax.axis_index(LON)
    dev = (lat * 32 + lon).astype(jnp.int32).reshape(1)
    forward_np, inverse_np = dft_tables()
    forward_table = jnp.asarray(forward_np)
    inverse_table = jnp.asarray(inverse_np)

    msg, flux, flux_west = norm_and_flux(atm_state, atm_gain, flux_weight)
    rows = exchange(msg, LON)

    flux_east = lax.ppermute(flux_west, LON, ring(32, -1))
    away = intersection_point - POINTS
    points = jnp.where(
        away < 0, intersection_point, POINTS + (away // COLS) * 16 + away % COLS
    ).reshape(CELLS, KOV)
    wet_col = wet.astype(F32).reshape(CELLS, 1)
    own, to_east = scatter(
        ocean_state, surface_weight, wet_col, points.T, return_intersection.reshape(CELLS, KOV).T
    )
    analysis, synthesis = legendre_tables(after(dev, msg))
    mix = gather(
        flux, flux_east, ocean_state, wet_col, ocean_in, points, intersection_weight.reshape(CELLS, KOV)
    )
    rows = after(rows, mix, analysis, to_east)

    waves = dft(rows, forward_table)
    by_order = exchange(waves, ALL)

    mix_2, to_east = lax.optimization_barrier((mix, to_east, waves))[:2]
    from_west = lax.ppermute(to_east, LON, ring(32, 1))
    west = lax.ppermute(mix_2[:, 13:], LON, ring(32, 1))
    east = lax.ppermute(mix_2[:, :3], LON, ring(32, -1))
    wide = lambda rows_of: jnp.concatenate(
        [west[rows_of], mix_2[rows_of], east[rows_of]], axis=1
    )
    top = wide(slice(13, 16))
    south = lax.ppermute(top, LAT, [(i, i + 1) for i in range(7)])
    north = lax.ppermute(wide(slice(0, 3)), LAT, [(i + 1, i) for i in range(7)])
    fold = lax.ppermute(top[::-1, ::-1], LON, [(i, 31 - i) for i in range(32)])
    north = jnp.where(lat == 7, fold, north)
    ocean_next, grads = ocean(
        mix_2, west, east, south, north, depth_kernel, ocean_gain, ocean_up, ocean_down, wet_col, ocean_cot
    )
    by_order = after(by_order, grads)

    mixed = spectral_mix(by_order, analysis, synthesis, spec_weight)
    by_row = exchange(mixed, ALL)

    grads = after(grads, mixed)
    plane = sum_parts(exchange(grads, PLANE), "plane_sum")
    column = sum_parts(spread(plane, COLUMN, 8), "column_sum")
    by_row = after(by_row, column)

    grid = inverse_dft(by_row, inverse_table)
    spectral = exchange(grid, LON)

    grad_up, grad_down = unpack(spread(after(column, grid), PLANE, 32))
    spectral = after(spectral, grad_up)

    atm_next = finish(atm_state, spectral, own, from_west, mlp_in, mlp_out, return_weight)
    return (atm_next, ocean_next, grad_up, grad_down)


LAT = ("zh", "core")
LON = ("y", "zl", "x")
ALL = LAT + LON
PLANE = ("core", "y", "x")
COLUMN = ("zh", "zl")


def solution(mesh):
    fine = Mesh(mesh.devices.reshape(4, 2, 4, 2, 4), ALL)
    block = P(LAT, LON)
    whole = P()
    in_specs = (block,) + (whole,) * 6 + (block,) * 2 + (whole,) * 6 + (block,) * 4
    out_specs = (block, block, whole, whole)
    return jax.shard_map(local, mesh=fine, in_specs=in_specs, out_specs=out_specs, check_vma=False)
```

time: 728 us -> 298 us (0.41)
  waiting for transfers between devices: 270 us -> 106 us
  other arithmetic: 114 us -> 0.12 us
  local copies, waits for them, and re-layouts: 99.5 us -> 29.5 us
  Pallas kernels: 0 us -> 37.6 us
  matrix products: 33.6 us -> 0 us
  starting transfers between devices: 81.5 us -> 59 us
  blocking collectives: 85.5 us -> 63.6 us
  loops' own time: 19.8 us -> 0 us
  between operations: 15.3 us -> 1.09 us
    psum x1 -> x0, waiting for transfers between devices: 241 us -> none  [local(): grad_up, grad_down = lax.psum((up_local, down_local), ('lat', 'lon'))]
    all_gather x1 -> x0, blocking collectives: 85.5 us -> none  [local(): top_band = lax.all_gather(ocean_mix[o_rows - 3:], 'lon', axis=1, tiled=True)]
    all_to_all x0 -> x3, blocking collectives: none -> 63.6 us  [exchange(): return lax.all_to_all(x, axes, split_axis=0, concat_axis=0, tiled=True)]
    ppermute x6 -> x7, waiting for transfers between devices: 0.1 us -> 49.1 us  [the longest x1 18.9 us: local(): east = lax.ppermute(mix_2[:, :3], LON, ring(32, -1))]
    while x496 -> x0, other arithmetic: 42.7 us -> none
    pallas_call x0 -> x12, Pallas kernels: none -> 37.6 us  [the longest x1 5.61 us: finish(): pl.pallas_call(finish_kernel, grid=(ROWS // step,), out_shape=jax.ShapeDt...]
    dot_general x14 -> x0, matrix products: 33.6 us -> none  [the longest x1 6.95 us: local(): update = jnp.dot(activation, mlp_out, preferred_element_type=jnp.float32)]
    all_to_all x6 -> x4, waiting for transfers between devices: 29.3 us -> 57 us  [exchange(): return lax.all_to_all(x, axes, split_axis=0, concat_axis=0, tiled=True)]
  transfers between devices with their start and end apart: 13 -> 11, of which waited for: 5 -> 7; matrix products, arithmetic and copies ran while one was open for 27% -> 1% of each run, Pallas kernels for 0% -> 5%
where the time goes in v1:
time: 298 us; the launch traced here: 297 us
  waiting for transfers between devices  106 us (36%)
  blocking collectives  63.6 us (21%)
  starting transfers between devices  59 us (20%)
  Pallas kernels  37.6 us (13%)
  local copies, waits for them, and re-layouts  29.5 us (10%)
    all_to_all x3, blocking collectives, exchange(): return lax.all_to_all(x, axes, split_axis=0, concat_axis=0, tiled=True)  63.6 us
    all_to_all x4, waiting for transfers between devices, exchange(): return lax.all_to_all(x, axes, split_axis=0, concat_axis=0, tiled=True)  57 us
    all_to_all x4, starting transfers between devices, exchange(): return lax.all_to_all(x, axes, split_axis=0, concat_axis=0, tiled=True)  38.6 us
    unnamed x92, local copies, waits for them, and re-layouts  27.4 us
    ppermute x1, waiting for transfers between devices, local(): east = lax.ppermute(mix_2[:, :3], LON, ring(32, -1))  18.9 us
    ppermute x1, waiting for transfers between devices, local(): west = lax.ppermute(mix_2[:, 13:], LON, ring(32, 1))  13.6 us
    ppermute x1, waiting for transfers between devices, local(): flux_east = lax.ppermute(flux_west, LON, ring(32, -1))  9.71 us
    ppermute x1, waiting for transfers between devices, local(): from_west = lax.ppermute(to_east, LON, ring(32, 1))  6.08 us
  transfers between devices with their start and end apart: 11, of which 7 were waited for; matrix products, arithmetic and copies ran while one was open for 1% of the time, Pallas kernels for 5%

profile of v1, /device:TPU:1, one launch (start us, length us, event | category | flops | bytes accessed | tf_op | source)
XLA Modules:
  0.0 297.0 jit_solution(3928078387320711453)
XLA Ops:
  7.7 9.6 %all-to-all-start = ((bf16[32,32,768]{2,1,0:T(8,128)(2,1)}), bf16[32,32,768]{2,1,0:T(8,128)(2,1)}, u32[]{:S(2)}, u32[]{:S(2)}) async-start(bf16[32,32,768]{2,1,0:T(8,128)(2,1)} %copy-done.1), calls=%async_computation | async-start | bytes 3145728 | tf_op jit(solution)/shard_map/all_to_all | solution.py:463
  17.3 5.6 %collective-permute-start = (bf16[1024,128]{1,0:T(8,128)(2,1)}, bf16[1024,128]{1,0:T(8,128)(2,1)}, u32[]{:S(2)}, u32[]{:S(2)}) collective-permute-start(bf16[1024,128]{1,0:T(8,128)(2,1)} %get-tuple-element.26), channel_id=1, source_target_pairs={{0,31},{1,0},{2,1},{3,2},{4,3},{5,4},{6,5},{7,6},{8,7},{9,8},{10,9... | collective-permute-start | bytes 786440 | tf_op jit(solution)/shard_map/ppermute | solution.py:509
  24.4 3.5 %legendre.1 = (bf16[2,512,512]{2,1,0:T(8,128)(2,1)S(1)}, bf16[2,512,512]{2,1,0:T(8,128)(2,1)S(1)}) custom-call(s32[1]{0:T(128)} %bitcast.1.dev_ref, f32[256,4,512]{2,1,0:T(4,128)S(1)} %copy-done, f32[256,8,128]{2,1,0:T(8,128)S(1)} %copy-done.11, f32[8,128]{1,0:T(8,128)S(1)} %copy-done.19, f32[4,128]{1,0:T(4,128)S(1)} %copy-done.20), custom_call_target="tpu_custom_call" | custom-call | flops 10000000 | bytes 4000000 | tf_op jit(solution)/shard_map/legendre/pallas_call | solution.py:116
  32.2 9.7 %collective-permute-done.east_ref = bf16[1024,128]{1,0:T(8,128)(2,1)} collective-permute-done((bf16[1024,128]{1,0:T(8,128)(2,1)}, bf16[1024,128]{1,0:T(8,128)(2,1)}, u32[]{:S(2)}, u32[]{:S(2)}) %collective-permute-start) | collective-permute-done | bytes 262176 | tf_op jit(solution)/shard_map/ppermute | solution.py:509
  41.9 2.7 gather.1.mix_ref
  46.3 3.7 %dft.1 = bf16[256,8,384]{2,1,0:T(8,128)(2,1)S(1)} custom-call(bf16[32,32,768]{2,1,0:T(8,128)(2,1)} %all-to-all-done.x_ref, bf16[1024,1024]{1,0:T(8,128)(2,1)S(1)} %copy-done.37), custom_call_target="tpu_custom_call" | custom-call | flops 1700000000 | bytes 6000000 | tf_op jit(solution)/shard_map/dft/pallas_call | solution.py:206
  51.1 16.1 %all-to-all-start.1 = ((bf16[256,8,384]{2,1,0:T(8,128)(2,1)}), bf16[256,8,384]{2,1,0:T(8,128)(2,1)}, u32[]{:S(2)}, u32[]{:S(2)}) async-start(bf16[256,8,384]{2,1,0:T(8,128)(2,1)} %copy-done.2), calls=%async_computation.1 | async-start | bytes 3145728 | tf_op jit(solution)/shard_map/all_to_all | solution.py:463
  67.3 6.1 %collective-permute-start.2 = (bf16[16,3,256]{2,1,0:T(4,128)(2,1)S(1)}, bf16[16,3,256]{2,1,0:T(4,128)(2,1)S(1)}, u32[]{:S(2)}, u32[]{:S(2)}) collective-permute-start(bf16[16,3,256]{2,1,0:T(4,128)(2,1)S(1)} %get-tuple-element.46), channel_id=1, source_target_pairs={{0,31},{1,0},{2,1},{3,2},{4,3},{5,4},{6,5},{7,6},{8,7},{9,8},{10,9... | collective-permute-start | bytes 73736 | tf_op jit(solution)/shard_map/ppermute | solution.py:530
  73.4 18.9 %collective-permute-done.2.east_ref = bf16[16,3,256]{2,1,0:T(4,128)(2,1)S(1)} collective-permute-done((bf16[16,3,256]{2,1,0:T(4,128)(2,1)S(1)}, bf16[16,3,256]{2,1,0:T(4,128)(2,1)S(1)}, u32[]{:S(2)}, u32[]{:S(2)}) %collective-permute-start.2) | collective-permute-done | bytes 24608 | tf_op jit(solution)/shard_map/ppermute | solution.py:530
  92.3 13.6 %collective-permute-done.1.west_ref = bf16[16,3,256]{2,1,0:T(4,128)(2,1)S(1)} collective-permute-done((bf16[16,3,256]{2,1,0:T(4,128)(2,1)S(1)}, bf16[16,3,256]{2,1,0:T(4,128)(2,1)S(1)}, u32[]{:S(2)}, u32[]{:S(2)}) %collective-permute-start.1) | collective-permute-done | bytes 24608 | tf_op jit(solution)/shard_map/ppermute | solution.py:529
  106.2 2.8 collective-permute-start.5
  109.1 4.5 %collective-permute-start.3 = (bf16[3,22,256]{2,1,0:T(8,128)(2,1)S(1)}, bf16[3,22,256]{2,1,0:T(8,128)(2,1)S(1)}, u32[]{:S(2)}, u32[]{:S(2)}) collective-permute-start(bf16[3,22,256]{2,1,0:T(8,128)(2,1)S(1)} %pad_maximum_fusion), channel_id=1, source_target_pairs={{0,32},{32,64},{64,96},{96,128},{128,160},{160,192},{192,224},{1,3... | collective-permute-start | bytes 101384 | tf_op jit(solution)/shard_map/ppermute | solution.py:535
  115.3 4.2 %ocean.1 = (bf16[16,16,256]{2,1,0:T(8,128)(2,1)}, bf16[32,64,256]{2,1,0:T(8,128)(2,1)S(1)}) custom-call(bf16[16,16,256]{2,1,0:T(8,128)(2,1)S(1)} %copy-done.15, bf16[16,3,256]{2,1,0:T(4,128)(2,1)S(1)} %collective-permute-done.1.west_ref, bf16[16,3,256]{2,1,0:T(4,128)(2,1)S(1)} %collective-permute-done.2.east_ref, ...), custom_call_target="tpu_custom_call" | custom-call | flops 700000000 | bytes 4000000 | tf_op jit(solution)/shard_map/ocean/pallas_call | solution.py:417
  123.1 5.4 %spectral_mix.1 = bf16[256,8,384]{2,1,0:T(8,128)(2,1)S(1)} custom-call(bf16[256,8,384]{2,1,0:T(8,128)(2,1)} %all-to-all-done.1.w_ref, bf16[2,512,512]{2,1,0:T(8,128)(2,1)S(1)} %copy-done.22, bf16[2,512,512]{2,1,0:T(8,128)(2,1)S(1)} %copy-done.24, bf16[2,384,384]{2,1,0:T(8,128)(2,1)S(1)} %copy-done.25), custom_call_target="tpu_custom_call" | custom-call | flops 2900000000 | bytes 6000000 | tf_op jit(solution)/shard_map/spectral_mix/pallas_call | solution.py:265
  129.6 21.0 %all_to_all.35.parts_ref = bf16[32,64,256]{2,1,0:T(8,128)(2,1)} all-to-all(bf16[32,64,256]{2,1,0:T(8,128)(2,1)S(1)} %get-tuple-element.35), channel_id=1, replica_groups=mesh['zh'=4,'core'=2,'y'=4,'zl'=2,'x'=4] {'core','y','x'}, dimensions={0} | all-to-all | bytes 2097152 | tf_op jit(solution)/shard_map/all_to_all | solution.py:463
  153.4 20.2 %all_to_all.36.parts_ref = bf16[8,64,256]{2,1,0:T(8,128)(2,1)} all-to-all(bf16[8,64,256]{2,1,0:T(8,128)(2,1)S(1)} %broadcast_in_dim.4), channel_id=1, replica_groups=mesh['zh'=4,'core'=2,'y'=4,'zl'=2,'x'=4] {'zh','zl'}, dimensions={0} | all-to-all | bytes 524288 | tf_op jit(solution)/shard_map/all_to_all | solution.py:463
  173.7 8.2 %all-to-all-start.2 = ((bf16[256,8,384]{2,1,0:T(8,128)(2,1)}), bf16[256,8,384]{2,1,0:T(8,128)(2,1)S(1)}, u32[]{:S(2)}, u32[]{:S(2)}) async-start(bf16[256,8,384]{2,1,0:T(8,128)(2,1)} %copy-done.6), calls=%async_computation.2 | async-start | bytes 3145728 | tf_op jit(solution)/shard_map/all_to_all | solution.py:463
  183.5 40.1 %all-to-all-done.2.w_ref = bf16[256,8,384]{2,1,0:T(8,128)(2,1)S(1)} async-done(((bf16[256,8,384]{2,1,0:T(8,128)(2,1)}), bf16[256,8,384]{2,1,0:T(8,128)(2,1)S(1)}, u32[]{:S(2)}, u32[]{:S(2)}) %all-to-all-start.2) | async-done | bytes 1572896 | tf_op jit(solution)/shard_map/all_to_all | solution.py:463
  231.5 22.3 %all_to_all.37.parts_ref = bf16[32,64,256]{2,1,0:T(8,128)(2,1)} all-to-all(bf16[32,64,256]{2,1,0:T(8,128)(2,1)S(1)} %broadcast_in_dim.5), channel_id=1, replica_groups=mesh['zh'=4,'core'=2,'y'=4,'zl'=2,'x'=4] {'core','y','x'}, dimensions={0} | all-to-all | bytes 2097152 | tf_op jit(solution)/shard_map/all_to_all | solution.py:463
  253.9 4.7 %all-to-all-start.5 = ((bf16[32,32,768]{2,1,0:T(8,128)(2,1)}), bf16[32,32,768]{2,1,0:T(8,128)(2,1)S(1)}, u32[]{:S(2)}, u32[]{:S(2)}) async-start(bf16[32,32,768]{2,1,0:T(8,128)(2,1)} %copy-done.5), calls=%async_computation.5 | async-start | bytes 3145728 | tf_op jit(solution)/shard_map/all_to_all | solution.py:463
  259.9 2.6 unpack.1
  262.5 16.9 %all-to-all-done.5.s_ref = bf16[32,32,768]{2,1,0:T(8,128)(2,1)S(1)} async-done(((bf16[32,32,768]{2,1,0:T(8,128)(2,1)}), bf16[32,32,768]{2,1,0:T(8,128)(2,1)S(1)}, u32[]{:S(2)}, u32[]{:S(2)}) %all-to-all-start.5) | async-done | bytes 1572896 | tf_op jit(solution)/shard_map/all_to_all | solution.py:463
  280.6 6.1 %collective-permute-done.6.west_ref = bf16[1024,128]{1,0:T(8,128)(2,1)S(1)} collective-permute-done((bf16[1024,128]{1,0:T(8,128)(2,1)S(1)}, bf16[1024,128]{1,0:T(8,128)(2,1)S(1)}, u32[]{:S(2)}, u32[]{:S(2)}) %collective-permute-start.6) | collective-permute-done | bytes 262176 | tf_op jit(solution)/shard_map/ppermute | solution.py:528
  291.4 5.6 %finish.1 = bf16[64,32,384]{2,1,0:T(8,128)(2,1)} custom-call(bf16[64,32,384]{2,1,0:T(8,128)(2,1)S(1)} %copy-done.10, bf16[32,32,768]{2,1,0:T(8,128)(2,1)S(1)} %copy-done.4, bf16[2048,128]{1,0:T(8,128)(2,1)S(1)} %copy-done.39, bf16[1024,128]{1,0:T(8,128)(2,1)S(1)} %collective-permute-done.6.west_ref, bf16[384,768]{1,0:T(8,128)(2,1)S(1)} %copy-done.26, ...), custom_call_target="tpu_custom_call" | custom-call | flops 2700000000 | bytes 6000000 | tf_op jit(solution)/shard_map/finish/pallas_call | solution.py:302
  (124 shorter events, 41.6 us)
Async XLA Ops:
  3.6 19.3 %copy-start.44 = (s32[16,16]{1,0:T(8,128)S(1)}, s32[16,16]{1,0:T(8,128)}, u32[]{:S(2)}) copy-start(s32[16,16]{1,0:T(8,128)} %param.33) | copy-start | bytes 3076
  7.7 16.7 %copy-start.19 = (f32[8,128]{1,0:T(8,128)S(1)}, f32[8,128]{1,0:T(8,128)}, u32[]{:S(2)}) copy-start(f32[8,128]{1,0:T(8,128)} %constant.79.clone.cos_ref) | copy-start | bytes 12292
  7.7 16.7 %copy-start.20 = (f32[4,128]{1,0:T(4,128)S(1)}, f32[4,128]{1,0:T(4,128)}, u32[]{:S(2)}) copy-start(f32[4,128]{1,0:T(4,128)} %constant.80.clone.quad_ref) | copy-start | bytes 6148
  7.7 37.0 %all-to-all-start = ((bf16[32,32,768]{2,1,0:T(8,128)(2,1)}), bf16[32,32,768]{2,1,0:T(8,128)(2,1)}, u32[]{:S(2)}, u32[]{:S(2)}) async-start(bf16[32,32,768]{2,1,0:T(8,128)(2,1)} %copy-done.1), calls=%async_computation | async-start | bytes 3145728 | tf_op jit(solution)/shard_map/all_to_all | solution.py:463
  17.3 24.6 %collective-permute-start = (bf16[1024,128]{1,0:T(8,128)(2,1)}, bf16[1024,128]{1,0:T(8,128)(2,1)}, u32[]{:S(2)}, u32[]{:S(2)}) collective-permute-start(bf16[1024,128]{1,0:T(8,128)(2,1)} %get-tuple-element.26), channel_id=1, source_target_pairs={{0,31},{1,0},{2,1},{3,2},{4,3},{5,4},{6,5},{7,6},{8,7},{9,8},{10,9... | collective-permute-start | bytes 786440 | tf_op jit(solution)/shard_map/ppermute | solution.py:509
  24.4 17.5 %copy-start.13 = (bf16[2048,128]{1,0:T(8,128)(2,1)S(1)}, bf16[2048,128]{1,0:T(8,128)(2,1)}, u32[]{:S(2)}) copy-start(bf16[2048,128]{1,0:T(8,128)(2,1)} %copy-done.12) | copy-start | bytes 1572868
  24.4 17.5 %copy-start.18 = (bf16[128,256]{1,0:T(8,128)(2,1)S(1)}, bf16[128,256]{1,0:T(8,128)(2,1)}, u32[]{:S(2)}) copy-start(bf16[128,256]{1,0:T(8,128)(2,1)} %oin_ref.1) | copy-start | bytes 196612
  44.7 28.7 %copy-start.14 = (bf16[16,16,256]{2,1,0:T(8,128)(2,1)}, bf16[16,16,256]{2,1,0:T(8,128)(2,1)S(1)}, u32[]{:S(2)}) copy-start(bf16[16,16,256]{2,1,0:T(8,128)(2,1)S(1)} %gather.1.mix_ref) | copy-start | bytes 393220
  51.1 57.9 %copy-start.43 = (bf16[7,7,256]{2,1,0:T(8,128)(2,1)S(1)}, bf16[7,7,256]{2,1,0:T(8,128)(2,1)}, u32[]{:S(2)}) copy-start(bf16[7,7,256]{2,1,0:T(8,128)(2,1)} %param.35) | copy-start | bytes 75268
  51.1 63.3 %copy-start.28 = (bf16[256,1024]{1,0:T(8,128)(2,1)S(1)}, bf16[256,1024]{1,0:T(8,128)(2,1)}, u32[]{:S(2)}) copy-start(bf16[256,1024]{1,0:T(8,128)(2,1)} %up_ref.1) | copy-start | bytes 1572868
  51.1 63.3 %copy-start.29 = (bf16[1024,256]{1,0:T(8,128)(2,1)S(1)}, bf16[1024,256]{1,0:T(8,128)(2,1)}, u32[]{:S(2)}) copy-start(bf16[1024,256]{1,0:T(8,128)(2,1)} %down_ref.1) | copy-start | bytes 1572868
  51.1 63.3 %copy-start.32 = (bf16[16,16,256]{2,1,0:T(8,128)(2,1)S(1)}, bf16[16,16,256]{2,1,0:T(8,128)(2,1)}, u32[]{:S(2)}) copy-start(bf16[16,16,256]{2,1,0:T(8,128)(2,1)} %cot_ref.1) | copy-start | bytes 393220
  51.1 63.3 %copy-start.35 = (f32[256]{0:T(256)S(1)}, f32[256]{0:T(256)}, u32[]{:S(2)}) copy-start(f32[256]{0:T(256)} %param.36) | copy-start | bytes 3076
  51.1 68.4 %all-to-all-start.1 = ((bf16[256,8,384]{2,1,0:T(8,128)(2,1)}), bf16[256,8,384]{2,1,0:T(8,128)(2,1)}, u32[]{:S(2)}, u32[]{:S(2)}) async-start(bf16[256,8,384]{2,1,0:T(8,128)(2,1)} %copy-done.2), calls=%async_computation.1 | async-start | bytes 3145728 | tf_op jit(solution)/shard_map/all_to_all | solution.py:463
  67.3 25.0 %collective-permute-start.2 = (bf16[16,3,256]{2,1,0:T(4,128)(2,1)S(1)}, bf16[16,3,256]{2,1,0:T(4,128)(2,1)S(1)}, u32[]{:S(2)}, u32[]{:S(2)}) collective-permute-start(bf16[16,3,256]{2,1,0:T(4,128)(2,1)S(1)} %get-tuple-element.46), channel_id=1, source_target_pairs={{0,31},{1,0},{2,1},{3,2},{4,3},{5,4},{6,5},{7,6},{8,7},{9,8},{10,9... | collective-permute-start | bytes 73736 | tf_op jit(solution)/shard_map/ppermute | solution.py:530
  73.3 32.5 %collective-permute-start.1 = (bf16[16,3,256]{2,1,0:T(4,128)(2,1)S(1)}, bf16[16,3,256]{2,1,0:T(4,128)(2,1)S(1)}, u32[]{:S(2)}, u32[]{:S(2)}) collective-permute-start(bf16[16,3,256]{2,1,0:T(4,128)(2,1)S(1)} %get-tuple-element.47), channel_id=1, source_target_pairs={{0,1},{1,2},{2,3},{3,4},{4,5},{5,6},{6,7},{7,8},{8,9},{9,10},{10,1... | collective-permute-start | bytes 73736 | tf_op jit(solution)/shard_map/ppermute | solution.py:529
  106.0 7.5 %collective-permute-start.4 = (bf16[3,22,256]{2,1,0:T(8,128)(2,1)S(1)}, bf16[3,22,256]{2,1,0:T(8,128)(2,1)S(1)}, u32[]{:S(2)}, u32[]{:S(2)}) collective-permute-start(bf16[3,22,256]{2,1,0:T(8,128)(2,1)S(1)} %rev.3), channel_id=1, source_target_pairs={{0,31},{1,30},{2,29},{3,28},{4,27},{5,26},{6,25},{7,24},{8,23},{9,... | collective-permute-start | bytes 101384 | tf_op jit(solution)/shard_map/ppermute | solution.py:537
  106.2 7.4 %collective-permute-start.5 = (bf16[3,22,256]{2,1,0:T(8,128)(2,1)S(1)}, bf16[3,22,256]{2,1,0:T(8,128)(2,1)S(1)}, u32[]{:S(2)}, u32[]{:S(2)}) collective-permute-start(bf16[3,22,256]{2,1,0:T(8,128)(2,1)S(1)} %pad_maximum_fusion.1), channel_id=1, source_target_pairs={{32,0},{64,32},{96,64},{128,96},{160,128},{192,160},{224,192},{33,... | collective-permute-start | bytes 101384 | tf_op jit(solution)/shard_map/ppermute | solution.py:536
  109.1 5.3 %collective-permute-start.3 = (bf16[3,22,256]{2,1,0:T(8,128)(2,1)S(1)}, bf16[3,22,256]{2,1,0:T(8,128)(2,1)S(1)}, u32[]{:S(2)}, u32[]{:S(2)}) collective-permute-start(bf16[3,22,256]{2,1,0:T(8,128)(2,1)S(1)} %pad_maximum_fusion), channel_id=1, source_target_pairs={{0,32},{32,64},{64,96},{96,128},{128,160},{160,192},{192,224},{1,3... | collective-permute-start | bytes 101384 | tf_op jit(solution)/shard_map/ppermute | solution.py:535
  173.7 50.0 %all-to-all-start.2 = ((bf16[256,8,384]{2,1,0:T(8,128)(2,1)}), bf16[256,8,384]{2,1,0:T(8,128)(2,1)S(1)}, u32[]{:S(2)}, u32[]{:S(2)}) async-start(bf16[256,8,384]{2,1,0:T(8,128)(2,1)} %copy-done.6), calls=%async_computation.2 | async-start | bytes 3145728 | tf_op jit(solution)/shard_map/all_to_all | solution.py:463
  253.9 32.8 %copy-start.26 = (bf16[384,768]{1,0:T(8,128)(2,1)S(1)}, bf16[384,768]{1,0:T(8,128)(2,1)}, u32[]{:S(2)}) copy-start(bf16[384,768]{1,0:T(8,128)(2,1)} %w1_ref.1) | copy-start | bytes 1769476
  253.9 32.8 %copy-start.27 = (bf16[768,384]{1,0:T(8,128)(2,1)S(1)}, bf16[768,384]{1,0:T(8,128)(2,1)}, u32[]{:S(2)}) copy-start(bf16[768,384]{1,0:T(8,128)(2,1)} %w2_ref.1) | copy-start | bytes 1769476
  253.9 25.5 %all-to-all-start.5 = ((bf16[32,32,768]{2,1,0:T(8,128)(2,1)}), bf16[32,32,768]{2,1,0:T(8,128)(2,1)S(1)}, u32[]{:S(2)}, u32[]{:S(2)}) async-start(bf16[32,32,768]{2,1,0:T(8,128)(2,1)} %copy-done.5), calls=%async_computation.5 | async-start | bytes 3145728 | tf_op jit(solution)/shard_map/all_to_all | solution.py:463
  258.6 28.1 %collective-permute-start.6 = (bf16[1024,128]{1,0:T(8,128)(2,1)S(1)}, bf16[1024,128]{1,0:T(8,128)(2,1)S(1)}, u32[]{:S(2)}, u32[]{:S(2)}) collective-permute-start(bf16[1024,128]{1,0:T(8,128)(2,1)S(1)} %copy-done.31), channel_id=1, source_target_pairs={{0,1},{1,2},{2,3},{3,4},{4,5},{5,6},{6,7},{7,8},{8,9},{9,10},{10,1... | collective-permute-start | bytes 786440 | tf_op jit(solution)/shard_map/ppermute | solution.py:528
  (32 other events, 122.2 us)
